TPU v7x, 128 devices: a whole 4x4x4 slice. The times are simulated.
128 devices in a mesh: ox: 32 (over y, x, core), oy: 4 (over z).
Axes of the slice: x: 4, y: 4, z: 4, core: 2. Of those that a mesh axis runs over, the one named last changes fastest.
Arguments:
- state: float32 [4, 16, 32, 4096], P(None, None, 'oy', 'ox'), may hold values from -6 to 6
- levels: int32 [32, 4096], P('oy', 'ox'), may hold values from 0 to 16
- owner: int32 [262144, 1], P(('ox', 'oy')), may hold values from 0 to 127; in each aligned block of 2048 rows (0 to 2047, 2048 to 4095, ...) at most 48 rows name the same one
- atm_cell: int32 [262144], P(('ox', 'oy')), may hold values from 0 to 511
- area: float32 [262144], P(('ox', 'oy')), may hold values from 0.1 to 1
- air_temp: float32 [65536], P(('ox', 'oy')), may hold values from -6 to 6
- exchange_rate: float32 [65536], P(('ox', 'oy')), may hold values from 0.2 to 1
- rainfall: float32 [65536], P(('ox', 'oy')), may hold values from -3 to 3
Outputs:
- next_state: float32 [4, 16, 32, 4096], P(None, None, 'oy', 'ox')
Inputs may be any that keep to these rules, and one draw needn't show every extreme that they name: Of the 2048 exchange-grid cells of one device, at most 48 name the same owner.
All inputs are finite; a program needn't handle non-finite values.
Results may differ from a plain program's by a relative error of at most 0.0003.
Values sent between devices are 32-bit elements; how exact they have to be, the bound alone decides.
A program may use at most 64 MiB of HBM per device.

v0:
```python
import math

import jax
import jax.numpy as jnp
from jax import lax
from jax.sharding import PartitionSpec as P

EDDY_KAPPA = 0.1
VISC = 0.1
STEP = 0.2
SEA_TOP_PLANE = 0.5


def extended(block, sides, width, periodic):
    for axis, dim in sides:
        count = lax.axis_size(axis)
        forward = [(i, i + 1) for i in range(count - 1)]
        if periodic:
            forward.append((count - 1, 0))
        backward = [(target, source) for source, target in forward]
        low = lax.ppermute(
            lax.slice_in_dim(block, block.shape[dim] - width, None, axis=dim), axis, forward
        )
        high = lax.ppermute(lax.slice_in_dim(block, 0, width, axis=dim), axis, backward)
        block = jnp.concatenate([low, block, high], axis=dim)
    return block


def middle_box_entry(field):
    return field[:, 1:-1, 1:-1]


def beside(field):
    return (field[:, 1:-1, 2:], field[:, 1:-1, :-2], field[:, 2:, 1:-1], field[:, :-2, 1:-1])


def distribute_across(field, submerged_indicator):
    middle = middle_box_entry(field)
    summed = jnp.zeros_like(middle)
    for neighbour, wet_near in zip(beside(field), beside(submerged_indicator)):
        summed = summed + wet_near * (neighbour - middle)
    return middle_box_entry(submerged_indicator) * summed


def diapycnal_blend(middle, submerged_halfway):
    empty = jnp.zeros_like(middle[:1])
    beneath = jnp.concatenate([middle[1:], empty], 0)
    overhead = jnp.concatenate([empty, middle[:-1]], 0)
    wet_beneath = jnp.concatenate([submerged_halfway[1:], empty], 0)
    wet_overhead = jnp.concatenate([empty, submerged_halfway[:-1]], 0)
    return submerged_halfway * (
        wet_beneath * (beneath - middle) + wet_overhead * (overhead - middle)
    )


def gradient(pressure, submerged_indicator, first, second):
    middle = middle_box_entry(pressure)
    near = beside(pressure)
    wet_near = beside(submerged_indicator)
    return 0.5 * (
        wet_near[first] * (near[first] - middle) + wet_near[second] * (middle - near[second])
    )


def advance(haloed_grid_array, coriolis, thermal_box, fresh_cell):
    stratum_total = (haloed_grid_array.shape[0] - 1) // 4
    depth_index = lax.broadcasted_iota(jnp.float32, (stratum_total, 1, 1), 0)
    submerged_indicator = (depth_index < haloed_grid_array[4 * stratum_total][None]).astype(
        jnp.float32
    )
    thermal_array = haloed_grid_array[0:stratum_total]
    brine_array = haloed_grid_array[stratum_total : 2 * stratum_total]
    u_vel = haloed_grid_array[2 * stratum_total : 3 * stratum_total]
    v_vel = haloed_grid_array[3 * stratum_total : 4 * stratum_total]
    seawater_heaviness = submerged_indicator * (0.8 * brine_array - 0.2 * thermal_array)
    pressure = 0.1 * jnp.cumsum(seawater_heaviness, 0)
    grad_x = gradient(pressure, submerged_indicator, 0, 1)
    grad_y = gradient(pressure, submerged_indicator, 2, 3)
    submerged_halfway = middle_box_entry(submerged_indicator)
    thermal_halfway = middle_box_entry(thermal_array)
    salt_mid = middle_box_entry(brine_array)
    u_mid = middle_box_entry(u_vel)
    v_mid = middle_box_entry(v_vel)
    next_thermal_array = submerged_halfway * (
        thermal_halfway
        + EDDY_KAPPA
        * (
            distribute_across(thermal_array, submerged_indicator)
            + diapycnal_blend(thermal_halfway, submerged_halfway)
        )
    )
    next_thermal_array = next_thermal_array.at[0].add(
        SEA_TOP_PLANE * submerged_halfway[0] * thermal_box
    )
    next_brine = submerged_halfway * (
        salt_mid
        + EDDY_KAPPA
        * (
            distribute_across(brine_array, submerged_indicator)
            + diapycnal_blend(salt_mid, submerged_halfway)
        )
    )
    next_brine = next_brine.at[0].add(SEA_TOP_PLANE * submerged_halfway[0] * fresh_cell)
    next_eastward_speed = submerged_halfway * (
        u_mid
        + STEP * (coriolis * v_mid - grad_x)
        + VISC * distribute_across(u_vel, submerged_indicator)
    )
    next_northward_speed = submerged_halfway * (
        v_mid
        + STEP * (-coriolis * u_mid - grad_y)
        + VISC * distribute_across(v_vel, submerged_indicator)
    )
    return jnp.stack([next_thermal_array, next_brine, next_eastward_speed, next_northward_speed], 0)


def slot_positions(target, devices):
    entries = target.shape[0]
    block_rows = math.gcd(entries, 512)
    chosen = (target[:, None] == jnp.arange(devices, dtype=jnp.int32)[None, :]).astype(jnp.bfloat16)
    tiles = chosen.reshape(entries // block_rows, block_rows, devices)
    row_id = lax.broadcasted_iota(jnp.int32, (block_rows, block_rows), 0)
    col_id = lax.broadcasted_iota(jnp.int32, (block_rows, block_rows), 1)
    lower = (row_id > col_id).astype(jnp.bfloat16)

    def advance_block(carry, tile):
        inner = jnp.dot(lower, tile, preferred_element_type=jnp.float32) + carry[None, :]
        return (carry + jnp.sum(tile.astype(jnp.float32), 0), inner)

    start_count = jnp.zeros((devices,), jnp.float32)
    _, before = lax.scan(advance_block, start_count, tiles)
    earlier = jnp.sum(before.reshape(entries, devices) * chosen.astype(jnp.float32), 1)
    return earlier.astype(jnp.int32)


def pick_rows(index, table):
    count = index.shape[0]
    block_rows = math.gcd(count, 512)
    columns = jnp.arange(table.shape[0], dtype=jnp.int32)

    def pick_block(part):
        onehot = (part[:, None] == columns[None, :]).astype(jnp.float32)
        return jnp.dot(
            onehot, table, precision=lax.Precision.HIGHEST, preferred_element_type=jnp.float32
        )

    picked = lax.map(pick_block, index.reshape(count // block_rows, block_rows))
    return picked.reshape(count, table.shape[1])


def sum_rows(index, values, segments):
    count = index.shape[0]
    block_rows = math.gcd(count, 512)
    columns = jnp.arange(segments, dtype=jnp.int32)

    def add_block(carry, pieces):
        part, rows = pieces
        onehot = (part[:, None] == columns[None, :]).astype(jnp.float32)
        term = lax.dot_general(
            onehot,
            rows,
            (((0,), (0,)), ((), ())),
            precision=lax.Precision.HIGHEST,
            preferred_element_type=jnp.float32,
        )
        return (carry + term, None)

    start = jnp.zeros((segments, values.shape[1]), jnp.float32)
    parts = (
        index.reshape(count // block_rows, block_rows),
        values.reshape(count // block_rows, block_rows, values.shape[1]),
    )
    total, _ = lax.scan(add_block, start, parts)
    return total


def per_device(state, levels, owner, atm_cell, area, air_temp, exchange_rate, rainfall):
    planes, depth_count, row_count, col_count = state.shape
    x_count = lax.axis_size("ox")
    y_count = lax.axis_size("oy")
    devices = x_count * y_count
    entries = owner.shape[0]
    capacity = max(2, 3 * entries // devices)
    atm_count = air_temp.shape[0]
    wet_top = (levels > 0).astype(jnp.float32)
    weights = area * jnp.repeat(wet_top.reshape(-1), 2)
    sea_temp = jnp.repeat(state[0, 0].reshape(-1), 2)
    sea_salt = jnp.repeat(state[1, 0].reshape(-1), 2)
    target = owner[:, 0]
    position = slot_positions(target, devices)
    flat_slot = target * capacity + position
    values = jnp.stack(
        [weights * sea_temp, weights * sea_salt, weights, atm_cell.astype(jnp.float32) + 1.0], 1
    )
    placed = sum_rows(flat_slot, values, devices * capacity)
    placed = placed - jnp.array([0.0, 0.0, 0.0, 1.0], jnp.float32)[None, :]
    outgoing = placed.reshape(devices, capacity, 4).transpose(0, 2, 1)
    arrived = lax.all_to_all(outgoing, ("ox", "oy"), split_axis=0, concat_axis=0, tiled=True)
    cell_ids = arrived[:, 3, :].reshape(-1)
    slot_cell = jnp.where(cell_ids < 0.0, atm_count, cell_ids.astype(jnp.int32))
    pooled = jnp.stack(
        [arrived[:, 0, :].reshape(-1), arrived[:, 1, :].reshape(-1), arrived[:, 2, :].reshape(-1)],
        1,
    )
    totals = sum_rows(slot_cell, pooled, atm_count)
    divisor = jnp.maximum(totals[:, 2], 1.0)
    heat_flux = exchange_rate * (air_temp - totals[:, 0] / divisor)
    fresh_flux = rainfall * (totals[:, 1] / divisor)
    slot_flux = pick_rows(slot_cell, jnp.stack([heat_flux, fresh_flux], 1))
    returning = slot_flux.reshape(devices, capacity, 2).transpose(0, 2, 1)
    landed = lax.all_to_all(returning, ("ox", "oy"), split_axis=0, concat_axis=0, tiled=True)
    landed_flat = landed.transpose(0, 2, 1).reshape(devices * capacity, 2)
    entry_flux = pick_rows(flat_slot, landed_flat)
    pair_area = area.reshape(row_count, col_count, 2)
    area_sum = jnp.sum(pair_area, -1)
    thermal_box = (
        jnp.sum(pair_area * entry_flux[:, 0].reshape(row_count, col_count, 2), -1) / area_sum
    )
    fresh_cell = (
        jnp.sum(pair_area * entry_flux[:, 1].reshape(row_count, col_count, 2), -1) / area_sum
    )
    stacked = jnp.concatenate(
        [
            state.reshape(planes * depth_count, row_count, col_count),
            levels.astype(jnp.float32)[None],
        ],
        0,
    )
    widened = extended(stacked, (("ox", 2),), 1, True)
    haloed_grid_array = extended(widened, (("oy", 1),), 1, False)
    top_row = stacked[:, row_count - 1, :]
    plane_total = top_row.shape[0]
    pieces = top_row.reshape(plane_total, x_count, col_count // x_count)
    spread_out = lax.all_to_all(pieces, "ox", split_axis=1, concat_axis=1, tiled=True)
    reordered = jnp.flip(spread_out, 1)
    returned = lax.all_to_all(reordered, "ox", split_axis=1, concat_axis=1, tiled=True)
    mirrored = jnp.flip(returned.reshape(plane_total, col_count), 1)
    parity = jnp.concatenate(
        [
            jnp.ones((2 * depth_count,), jnp.float32),
            -jnp.ones((2 * depth_count,), jnp.float32),
            jnp.ones((1,), jnp.float32),
        ],
        0,
    )
    fold_row = mirrored * parity[:, None]
    is_top = lax.axis_index("oy") == y_count - 1
    current = haloed_grid_array[:, row_count + 1, 1 : col_count + 1]
    haloed_grid_array = haloed_grid_array.at[:, row_count + 1, 1 : col_count + 1].set(
        jnp.where(is_top, fold_row, current)
    )
    row_index = (lax.axis_index("oy") * row_count + jnp.arange(row_count, dtype=jnp.int32)).astype(
        jnp.float32
    )
    coriolis = 0.2 + 0.8 * row_index[:, None] / (row_count * y_count)
    return advance(haloed_grid_array, coriolis, thermal_box, fresh_cell)


def solution(mesh):
    in_specs = (
        P(None, None, "oy", "ox"),
        P("oy", "ox"),
        P(("ox", "oy"), None),
        P(("ox", "oy")),
        P(("ox", "oy")),
        P(("ox", "oy")),
        P(("ox", "oy")),
        P(("ox", "oy")),
    )
    out_specs = P(None, None, "oy", "ox")
    return jax.shard_map(
        per_device, mesh=mesh, in_specs=in_specs, out_specs=out_specs, check_vma=False
    )
```

profile of v0, /device:TPU:1, one launch (start us, length us, event | category | flops | bytes accessed | tf_op | source)
XLA Modules:
  0.0 146.3 jit_solution(4577781443822621107)
XLA Ops:
  0.0 0.8 convert_element_type.50
  0.8 1.0 copy.20
  1.8 0.7 copy.21
  2.5 8.6 %all-to-all-start = ((f32[65,32,4]{0,2,1:T(4,128)}), f32[65,32,4]{0,2,1:T(4,128)S(1)}, u32[]{:S(2)}, u32[]{:S(2)}) async-start(f32[65,32,4]{0,2,1:T(4,128)} %bitcast.2), calls=%async_computation | async-start | bytes 131072 | tf_op jit(solution)/shard_map/all_to_all | solution.py:234
  11.3 1.7 %collective-permute-start = (f32[65,8,1]{2,0,1:T(8,128)S(1)}, f32[65,8,1]{2,0,1:T(8,128)S(1)}, u32[]{:S(2)}, u32[]{:S(2)}) collective-permute-start(f32[65,8,1]{2,0,1:T(8,128)S(1)} %get-tuple-element.332), channel_id=1, source_target_pairs={{0,4},{4,8},{8,12},{12,16},{16,20},{20,24},{24,28},{28,32},{32,36}... | collective-permute-start | bytes 6248 | tf_op jit(solution)/shard_map/ppermute | solution.py:21
  13.0 0.7 slice_bitcast_fusion.2
  14.3 0.7 reduce.34
  16.6 2.3 %while.62 = (s32[]{:T(128)}, f32[128]{0:T(128)S(1)}, f32[4,512,128]{1,2,0:T(8,128)S(1)}, bf16[4,512,128]{1,2,0:T(8,128)(2,1)S(1)}, s32[]{:T(128)}, /*index=5*/s32[]{:T(128)}) while((s32[]{:T(128)}, f32[128]{0:T(128)S(1)}, f32[4,512,128]{1,2,0:T(8,128)S(1)}, bf16[4,512,128]{1,2,0:T(8,128)(2,1)S(1)}, s32[]{:T(128)}, ...), condition=%wide.region_2.3_spmd.clone, body=%wide.region_0.2_spmd.clone.sunk | while | flops 67829888 | bytes 1052763 | solution.py:131
  19.6 16.4 %while.63 = (s32[]{:T(128)}, f32[6144,4]{0,1:T(4,128)S(1)}, s32[4,512]{1,0:T(4,128)S(1)}, f32[4,512,4]{1,2,0:T(4,128)S(1)}, s32[]{:T(128)}, /*index=5*/s32[]{:T(128)}) while((s32[]{:T(128)}, f32[6144,4]{0,1:T(4,128)S(1)}, s32[4,512]{1,0:T(4,128)S(1)}, f32[4,512,4]{1,2,0:T(4,128)S(1)}, s32[]{:T(128)}, /*index=5*/s32[]{:T(128)}) %tuple.129), condition=%wide.region_5.6_spmd.clone, body=%wide.region_4.5_spmd.clone.sunk | while | flops 154189824 | bytes 211039 | solution.py:173
  19.6 4.1 %fusion.133 = f32[6144,4]{0,1:T(4,128)S(1)} fusion(s32[512]{0:T(512)S(1)} %bitcast.128, f32[6144,4]{0,1:T(4,128)S(1)} %get-tuple-element.498, pred[]{:T(512)S(6)} %compare.32, f32[4,512,4]{1,2,0:T(4,128)S(1)} %get-tuple-element.506, s32[]{:T(128)S(6)} %copy.68), kind=kOutput, calls=%fused_computation.26.clone.1 | convolution fusion | flops 154189824 | bytes 206853 | tf_op jit(solution)/shard_map/while/body/eval_jaxpr/dot_general | solution.py:159
  23.7 4.1 %fusion.133 = f32[6144,4]{0,1:T(4,128)S(1)} fusion(s32[512]{0:T(512)S(1)} %bitcast.128, f32[6144,4]{0,1:T(4,128)S(1)} %get-tuple-element.498, pred[]{:T(512)S(6)} %compare.32, f32[4,512,4]{1,2,0:T(4,128)S(1)} %get-tuple-element.506, s32[]{:T(128)S(6)} %copy.68), kind=kOutput, calls=%fused_computation.26.clone.1 | convolution fusion | flops 154189824 | bytes 206853 | tf_op jit(solution)/shard_map/while/body/eval_jaxpr/dot_general | solution.py:159
  27.8 4.1 %fusion.133 = f32[6144,4]{0,1:T(4,128)S(1)} fusion(s32[512]{0:T(512)S(1)} %bitcast.128, f32[6144,4]{0,1:T(4,128)S(1)} %get-tuple-element.498, pred[]{:T(512)S(6)} %compare.32, f32[4,512,4]{1,2,0:T(4,128)S(1)} %get-tuple-element.506, s32[]{:T(128)S(6)} %copy.68), kind=kOutput, calls=%fused_computation.26.clone.1 | convolution fusion | flops 154189824 | bytes 206853 | tf_op jit(solution)/shard_map/while/body/eval_jaxpr/dot_general | solution.py:159
  31.9 4.1 %fusion.133 = f32[6144,4]{0,1:T(4,128)S(1)} fusion(s32[512]{0:T(512)S(1)} %bitcast.128, f32[6144,4]{0,1:T(4,128)S(1)} %get-tuple-element.498, pred[]{:T(512)S(6)} %compare.32, f32[4,512,4]{1,2,0:T(4,128)S(1)} %get-tuple-element.506, s32[]{:T(128)S(6)} %copy.68), kind=kOutput, calls=%fused_computation.26.clone.1 | convolution fusion | flops 154189824 | bytes 206853 | tf_op jit(solution)/shard_map/while/body/eval_jaxpr/dot_general | solution.py:159
  36.3 3.5 %collective-permute-start.2 = (f32[65,1,130]{2,0,1:T(8,128)S(1)}, f32[65,1,130]{2,0,1:T(8,128)S(1)}, u32[]{:S(2)}, u32[]{:S(2)}) collective-permute-start(f32[65,1,130]{2,0,1:T(8,128)S(1)} %get-tuple-element.328), channel_id=1, source_target_pairs={{0,1},{1,2},{2,3},{4,5},{5,6},{6,7},{8,9},{9,10},{10,11},{12,13},{... | collective-permute-start | bytes 101408 | tf_op jit(solution)/shard_map/ppermute | solution.py:21
  39.8 1.3 collective-permute-start.3
  42.0 1.0 reshape.288
  43.6 7.8 %all-to-all-start.1 = ((f32[65,32,4]{0,2,1:T(4,128)}), f32[65,32,4]{0,2,1:T(4,128)S(1)}, u32[]{:S(2)}, u32[]{:S(2)}) async-start(f32[65,32,4]{0,2,1:T(4,128)} %rev.8), calls=%async_computation.1 | async-start | bytes 131072 | tf_op jit(solution)/shard_map/all_to_all | solution.py:236
  51.9 6.7 %all-to-all-done.1 = f32[65,32,4]{0,2,1:T(4,128)S(1)} async-done(((f32[65,32,4]{0,2,1:T(4,128)}), f32[65,32,4]{0,2,1:T(4,128)S(1)}, u32[]{:S(2)}, u32[]{:S(2)}) %all-to-all-start.1) | async-done | bytes 33312 | tf_op jit(solution)/shard_map/all_to_all | solution.py:236
  58.7 7.4 %all-to-all-start.2 = ((f32[128,1,192]{2,1,0:T(1,128)}), f32[128,1,192]{2,1,0:T(1,128)S(1)}, u32[]{:S(2)}, u32[]{:S(2)}) async-start(f32[128,1,192]{2,1,0:T(1,128)} %reshape.288), calls=%async_computation.2 | async-start | bytes 262144 | tf_op jit(solution)/shard_map/all_to_all | solution.py:198
  66.4 14.4 %scatter.4 = f32[65,10,130]{2,1,0:T(8,128)S(1)} dynamic-update-slice(f32[65,10,130]{2,1,0:T(8,128)S(1)} %copy.23, f32[65,1,128]{2,1,0:T(1,128)S(1)} %reshape.234, s32[]{:T(128)} %copy.92, s32[]{:T(128)} %constant.169.clone.1, s32[]{:T(128)} %constant.170.clone.1) | dynamic-update-slice | bytes 66564 | tf_op jit(solution)/shard_map/scatter | solution.py:249
  82.5 1.0 reduce.35
  84.9 6.4 %while.64 = (s32[]{:T(128)}, f32[512,3]{0,1:T(4,128)S(1)}, s32[12,512]{1,0:T(8,128)S(1)}, f32[12,512,3]{1,0,2:T(8,128)S(1)}, s32[]{:T(128)}, /*index=5*/s32[]{:T(128)}) while((s32[]{:T(128)}, f32[512,3]{0,1:T(4,128)S(1)}, s32[12,512]{1,0:T(8,128)S(1)}, f32[12,512,3]{1,0,2:T(8,128)S(1)}, s32[]{:T(128)}, /*index=5*/s32[]{:T(128)}) %tuple.132), condition=%wide.region_7.8_spmd.clone, body=%wide.region_6.7_spmd.clone.sunk | while | flops 9702403 | bytes 36959 | solution.py:173
  91.4 9.0 %while.60 = (s32[]{:T(128)}, f32[12,512,2]{1,0,2:T(8,128)S(1)}, s32[12,512]{1,0:T(8,128)S(1)}, f32[512,2]{0,1:T(2,128)S(1)}, s32[]{:T(128)}, /*index=5*/s32[]{:T(128)}) while((s32[]{:T(128)}, f32[12,512,2]{1,0,2:T(8,128)S(1)}, s32[12,512]{1,0:T(8,128)S(1)}, f32[512,2]{0,1:T(2,128)S(1)}, s32[]{:T(128)}, /*index=5*/s32[]{:T(128)}) %tuple.142), condition=%wide.region_9.10_spmd.clone, body=%wide.region_8.9_spmd.clone.sunk | while | flops 6553602 | bytes 30805 | solution.py:147
  100.5 0.8 copy.28
  101.2 9.8 %all-to-all-start.3 = ((f32[128,2,48]{2,1,0:T(2,128)}), f32[128,2,48]{2,1,0:T(2,128)S(1)}, u32[]{:S(2)}, u32[]{:S(2)}) async-start(f32[128,2,48]{2,1,0:T(2,128)} %copy.28), calls=%async_computation.3 | async-start | bytes 262144 | tf_op jit(solution)/shard_map/all_to_all | solution.py:211
  111.3 9.7 %all-to-all-done.3 = f32[128,2,48]{2,1,0:T(2,128)S(1)} async-done(((f32[128,2,48]{2,1,0:T(2,128)}), f32[128,2,48]{2,1,0:T(2,128)S(1)}, u32[]{:S(2)}, u32[]{:S(2)}) %all-to-all-start.3) | async-done | bytes 49184 | tf_op jit(solution)/shard_map/all_to_all | solution.py:211
  121.1 22.9 %while.61 = (s32[]{:T(128)}, f32[4,512,2]{1,2,0:T(2,128)S(1)}, s32[4,512]{1,0:T(4,128)S(1)}, f32[6144,2]{0,1:T(2,128)S(1)}, s32[]{:T(128)}) while((s32[]{:T(128)}, f32[4,512,2]{1,2,0:T(2,128)S(1)}, s32[4,512]{1,0:T(4,128)S(1)}, f32[6144,2]{0,1:T(2,128)S(1)}, s32[]{:T(128)}) %tuple.141), condition=%wide.region_11.12_spmd.clone, body=%wide.region_10.11_spmd.clone.sunk | while | flops 78643200 | bytes 59469 | solution.py:147
  121.1 5.7 %fusion.127 = f32[4,512,2]{1,2,0:T(2,128)S(1)} fusion(f32[4,512,2]{1,2,0:T(2,128)S(1)} %get-tuple-element.551, s32[]{:T(128)S(6)} %copy.86, f32[6144,2]{0,1:T(2,128)S(1)} %get-tuple-element.558, s32[512]{0:T(512)S(1)} %bitcast.129), kind=kOutput, calls=%fused_computation.13.clone.1 | convolution fusion | flops 78643200 | bytes 55300 | tf_op jit(solution)/shard_map/while/body/eval_jaxpr/dot_general | solution.py:143
  126.9 5.7 %fusion.127 = f32[4,512,2]{1,2,0:T(2,128)S(1)} fusion(f32[4,512,2]{1,2,0:T(2,128)S(1)} %get-tuple-element.551, s32[]{:T(128)S(6)} %copy.86, f32[6144,2]{0,1:T(2,128)S(1)} %get-tuple-element.558, s32[512]{0:T(512)S(1)} %bitcast.129), kind=kOutput, calls=%fused_computation.13.clone.1 | convolution fusion | flops 78643200 | bytes 55300 | tf_op jit(solution)/shard_map/while/body/eval_jaxpr/dot_general | solution.py:143
  132.6 5.7 %fusion.127 = f32[4,512,2]{1,2,0:T(2,128)S(1)} fusion(f32[4,512,2]{1,2,0:T(2,128)S(1)} %get-tuple-element.551, s32[]{:T(128)S(6)} %copy.86, f32[6144,2]{0,1:T(2,128)S(1)} %get-tuple-element.558, s32[512]{0:T(512)S(1)} %bitcast.129), kind=kOutput, calls=%fused_computation.13.clone.1 | convolution fusion | flops 78643200 | bytes 55300 | tf_op jit(solution)/shard_map/while/body/eval_jaxpr/dot_general | solution.py:143
  138.3 5.7 %fusion.127 = f32[4,512,2]{1,2,0:T(2,128)S(1)} fusion(f32[4,512,2]{1,2,0:T(2,128)S(1)} %get-tuple-element.551, s32[]{:T(128)S(6)} %copy.86, f32[6144,2]{0,1:T(2,128)S(1)} %get-tuple-element.558, s32[512]{0:T(512)S(1)} %bitcast.129), kind=kOutput, calls=%fused_computation.13.clone.1 | convolution fusion | flops 78643200 | bytes 55300 | tf_op jit(solution)/shard_map/while/body/eval_jaxpr/dot_general | solution.py:143
  145.6 0.7 pad_maximum_fusion.1
  (209 shorter events, 27.5 us)
Async XLA Ops:
  0.0 13.0 %copy-start.3 = (s32[8,128]{1,0:T(8,128)S(1)}, s32[8,128]{1,0:T(8,128)}, u32[]{:S(2)}) copy-start(s32[8,128]{1,0:T(8,128)} %param.26) | copy-start | bytes 12292
  0.0 14.3 %copy-start.4 = (s32[2048,1]{0,1:T(1,128)S(1)}, s32[2048,1]{0,1:T(1,128)}, u32[]{:S(2)}) copy-start(s32[2048,1]{0,1:T(1,128)} %param.27) | copy-start | bytes 24580
  0.0 15.0 %copy-start.5 = (s32[2048]{0:T(1024)S(1)}, s32[2048]{0:T(1024)}, u32[]{:S(2)}) copy-start(s32[2048]{0:T(1024)} %param.28) | copy-start | bytes 24580
  0.8 35.4 %copy-start = (f32[8,128]{1,0:T(8,128)}, f32[8,128]{1,0:T(8,128)S(1)}, u32[]{:S(2)}) copy-start(f32[8,128]{1,0:T(8,128)S(1)} %convert_element_type.50) | copy-start | bytes 12292
  2.5 40.4 %all-to-all-start = ((f32[65,32,4]{0,2,1:T(4,128)}), f32[65,32,4]{0,2,1:T(4,128)S(1)}, u32[]{:S(2)}, u32[]{:S(2)}) async-start(f32[65,32,4]{0,2,1:T(4,128)} %bitcast.2), calls=%async_computation | async-start | bytes 131072 | tf_op jit(solution)/shard_map/all_to_all | solution.py:234
  11.3 24.9 %collective-permute-start = (f32[65,8,1]{2,0,1:T(8,128)S(1)}, f32[65,8,1]{2,0,1:T(8,128)S(1)}, u32[]{:S(2)}, u32[]{:S(2)}) collective-permute-start(f32[65,8,1]{2,0,1:T(8,128)S(1)} %get-tuple-element.332), channel_id=1, source_target_pairs={{0,4},{4,8},{8,12},{12,16},{16,20},{20,24},{24,28},{28,32},{32,36}... | collective-permute-start | bytes 6248 | tf_op jit(solution)/shard_map/ppermute | solution.py:21
  13.0 23.2 %collective-permute-start.1 = (f32[65,8,1]{2,0,1:T(8,128)S(1)}, f32[65,8,1]{2,0,1:T(8,128)S(1)}, u32[]{:S(2)}, u32[]{:S(2)}) collective-permute-start(f32[65,8,1]{2,0,1:T(8,128)S(1)} %get-tuple-element.333), channel_id=1, source_target_pairs={{4,0},{8,4},{12,8},{16,12},{20,16},{24,20},{28,24},{32,28},{36,32}... | collective-permute-start | bytes 6248 | tf_op jit(solution)/shard_map/ppermute | solution.py:24
  18.8 0.7 copy-start.2
  19.6 16.4 %copy-start.10 = (f32[4]{0:T(128)S(1)}, f32[4]{0:T(128)}, u32[]{:S(2)}) copy-start(f32[4]{0:T(128)} %constant.194) | copy-start | bytes 52
  36.3 15.1 %copy-start.1 = (f32[8,128]{1,0:T(8,128)S(1)}, f32[8,128]{1,0:T(8,128)}, u32[]{:S(2)}) copy-start(f32[8,128]{1,0:T(8,128)} %copy-done) | copy-start | bytes 12292
  36.3 15.1 %collective-permute-start.2 = (f32[65,1,130]{2,0,1:T(8,128)S(1)}, f32[65,1,130]{2,0,1:T(8,128)S(1)}, u32[]{:S(2)}, u32[]{:S(2)}) collective-permute-start(f32[65,1,130]{2,0,1:T(8,128)S(1)} %get-tuple-element.328), channel_id=1, source_target_pairs={{0,1},{1,2},{2,3},{4,5},{5,6},{6,7},{8,9},{9,10},{10,11},{12,13},{... | collective-permute-start | bytes 101408 | tf_op jit(solution)/shard_map/ppermute | solution.py:21
  39.8 11.5 %collective-permute-start.3 = (f32[65,1,130]{2,0,1:T(8,128)S(1)}, f32[65,1,130]{2,0,1:T(8,128)S(1)}, u32[]{:S(2)}, u32[]{:S(2)}) collective-permute-start(f32[65,1,130]{2,0,1:T(8,128)S(1)} %get-tuple-element.329), channel_id=1, source_target_pairs={{1,0},{2,1},{3,2},{5,4},{6,5},{7,6},{9,8},{10,9},{11,10},{13,12},{... | collective-permute-start | bytes 101408 | tf_op jit(solution)/shard_map/ppermute | solution.py:24
  43.6 15.1 %all-to-all-start.1 = ((f32[65,32,4]{0,2,1:T(4,128)}), f32[65,32,4]{0,2,1:T(4,128)S(1)}, u32[]{:S(2)}, u32[]{:S(2)}) async-start(f32[65,32,4]{0,2,1:T(4,128)} %rev.8), calls=%async_computation.1 | async-start | bytes 131072 | tf_op jit(solution)/shard_map/all_to_all | solution.py:236
  51.7 14.5 %copy-start.9 = (f32[65]{0:T(128)S(1)}, f32[65]{0:T(128)}, u32[]{:S(2)}) copy-start(f32[65]{0:T(128)} %constant.167.clone.1) | copy-start | bytes 784
  58.7 23.3 %all-to-all-start.2 = ((f32[128,1,192]{2,1,0:T(1,128)}), f32[128,1,192]{2,1,0:T(1,128)S(1)}, u32[]{:S(2)}, u32[]{:S(2)}) async-start(f32[128,1,192]{2,1,0:T(1,128)} %reshape.288), calls=%async_computation.2 | async-start | bytes 262144 | tf_op jit(solution)/shard_map/all_to_all | solution.py:198
  84.6 6.7 %copy-start.6 = (f32[512]{0:T(512)S(1)}, f32[512]{0:T(512)}, u32[]{:S(2)}) copy-start(f32[512]{0:T(512)} %param.32) | copy-start | bytes 6148
  84.7 6.7 %copy-start.7 = (f32[512]{0:T(512)S(1)}, f32[512]{0:T(512)}, u32[]{:S(2)}) copy-start(f32[512]{0:T(512)} %param.31) | copy-start | bytes 6148
  84.7 6.7 %copy-start.8 = (f32[512]{0:T(512)S(1)}, f32[512]{0:T(512)}, u32[]{:S(2)}) copy-start(f32[512]{0:T(512)} %param.30) | copy-start | bytes 6148
  101.2 19.7 %all-to-all-start.3 = ((f32[128,2,48]{2,1,0:T(2,128)}), f32[128,2,48]{2,1,0:T(2,128)S(1)}, u32[]{:S(2)}, u32[]{:S(2)}) async-start(f32[128,2,48]{2,1,0:T(2,128)} %copy.28), calls=%async_computation.3 | async-start | bytes 262144 | tf_op jit(solution)/shard_map/all_to_all | solution.py:211
where the time goes:
time: 147 us; the launch traced here: 146 us
  matrix products  53.9 us (37%)
  starting transfers between devices  40 us (27%)
  local copies, waits for them, and re-layouts  27.9 us (19%)
  waiting for transfers between devices  16.4 us (11%)
  other arithmetic  6.62 us (5%)
    dot_general x16, matrix products, pick_block(): jnp.dot(onehot, table, precision=lax.Precision.HIGHEST, preferred_element...  30.4 us
    dot_general x16, matrix products, add_block(): lax.dot_general(onehot, rows, (((0,), (0,)), ((), ())), precision=lax.Pre...  22.3 us
    scatter x1, local copies, waits for them, and re-layouts, per_device(): haloed_grid_array.at[:, row_count + 1, 1:col_count + 1]  14.4 us
    all_to_all x1, starting transfers between devices, per_device(): lax.all_to_all(returning, ('ox', 'oy'), split_axis=0, concat_axis=0, tile...  9.76 us
    all_to_all x1, waiting for transfers between devices, per_device(): lax.all_to_all(returning, ('ox', 'oy'), split_axis=0, concat_axis=0, tile...  9.7 us
    all_to_all x1, starting transfers between devices, per_device(): lax.all_to_all(pieces, 'ox', split_axis=1, concat_axis=1, tiled=True)  8.59 us
    all_to_all x1, starting transfers between devices, per_device(): lax.all_to_all(reordered, 'ox', split_axis=1, concat_axis=1, tiled=True)  7.76 us
    all_to_all x1, starting transfers between devices, per_device(): lax.all_to_all(outgoing, ('ox', 'oy'), split_axis=0, concat_axis=0, tiled...  7.39 us
  transfers between devices with their start and end apart: 8, of which 2 were waited for; matrix products, arithmetic and copies ran while one was open for 28% of the time, Pallas kernels for 0%

commit v1 on v0

v1 whole, which is shorter than its diff:
```python
import jax
import jax.numpy as jnp
from jax import lax
from jax.experimental import pallas as pl
from jax.experimental.pallas import tpu as pltpu
from jax.sharding import PartitionSpec as P

NZ = 16
CY = 8
CX = 128
DEV = 128
N_OY = 4
TILES = 16
HALF = 64
SLOTS = 48
PLANES = 88
EDDY_KAPPA = 0.1
VISC = 0.1
STEP = 0.2
SEA_TOP = 0.5
F32 = jnp.float32
BF16 = jnp.bfloat16
LOGICAL = pl.DeviceIdType.LOGICAL


def hops(mask):
    ring = (0, 1, 2, 1)
    return 4 * (ring[mask & 3] + ring[(mask >> 3) & 3] + ring[(mask >> 5) & 3]) + ((mask >> 2) & 1)


PARTNERS = sorted(range(1, DEV), key=lambda mask: -hops(mask))


def split(value):
    high = value.astype(BF16).astype(F32)
    return high, value - high


def kernel(
    state, levels, owner, cell, area, air, rate, rain,
    out,
    st, lev, raw_own, raw_cell, raw_area, atm,
    z_own, z_cell, z_pos, z_area, z_val,
    chosen, slot_a, slot_b,
    out_slots, in_slots, out_flux, in_flux, flipped,
    rows, left, right,
    pres, north_out, south_out, halo_in, west_out, east_out, side_in,
    local_sem, out_sem, in_sem, halo_out_sem, halo_in_sem,
):
    ox, oy = lax.axis_index("ox"), lax.axis_index("oy")
    me = ox * N_OY + oy
    n_ox = DEV // N_OY

    loads = [
        pltpu.make_async_copy(source, target, local_sem.at[i])
        for i, (source, target) in enumerate(
            (
                (owner, raw_own), (cell, raw_cell), (area, raw_area), (levels, lev), (state, st),
                (air, atm.at[0, 0:4]), (air, atm.at[0, 4:8]),
                (rate, atm.at[1, 0:4]), (rate, atm.at[1, 4:8]),
                (rain, atm.at[2, 0:4]), (rain, atm.at[2, 4:8]),
            )
        )
    ]
    for copy in loads:
        copy.start()
    barrier = pltpu.get_barrier_semaphore()
    for mask in PARTNERS:
        pl.semaphore_signal(barrier, inc=1, device_id=me ^ mask, device_id_type=LOGICAL)
    for copy in loads:
        copy.wait()

    lane = lax.broadcasted_iota(jnp.int32, (8, 128), 1)
    sub = lax.broadcasted_iota(jnp.int32, (8, 128), 0)
    low_half = lane < HALF
    level = lev[...]

    for source, target in ((raw_own, z_own), (raw_cell, z_cell), (raw_area, z_area)):
        even, odd = source[pl.ds(0, 8, stride=2), :], source[pl.ds(1, 8, stride=2), :]
        for c in range(2):
            index = 2 * (lane & (HALF - 1)) + c
            target[pl.ds(8 * c, 8), :] = jnp.where(
                low_half,
                jnp.take_along_axis(even, index, axis=1),
                jnp.take_along_axis(odd, index, axis=1),
            )
    wet_top = (level > 0).astype(F32)
    temp_top, salt_top = st[0:8, :], st[128:136, :]
    for c in range(2):
        part = pl.ds(8 * c, 8)
        weight = z_area[part, :] * wet_top
        for i, value in enumerate(
            (weight * temp_top, weight * salt_top, weight, z_cell[part, :].astype(F32))
        ):
            high, low = split(value)
            z_val[2 * i, part, :] = high
            z_val[2 * i + 1, part, :] = low

    owner_row = lax.broadcasted_iota(jnp.int32, (DEV, 128), 0)

    def mark_owner(t, carry):
        columns = pl.ds(pl.multiple_of(t * 128, 128), 128)
        chosen[:, columns] = jnp.where(z_own[pl.ds(t, 1), :] == owner_row, 1.0, 0.0).astype(BF16)
        return carry

    lax.fori_loop(0, TILES, mark_owner, 0, unroll=4)

    upto = (
        lax.broadcasted_iota(jnp.int32, (256, 256), 0)
        <= lax.broadcasted_iota(jnp.int32, (256, 256), 1)
    )
    upto = jnp.where(upto, 1.0, 0.0).astype(BF16)
    seen = jnp.zeros((DEV, 1), F32)
    for b in range(TILES // 2):
        block = chosen[:, 256 * b : 256 * (b + 1)]
        count = jnp.dot(block, upto, preferred_element_type=F32)
        place = jnp.sum(block.astype(F32) * (count + seen), axis=0, keepdims=True) - 1.0
        z_pos[2 * b : 2 * b + 1, :] = place[:, :128]
        z_pos[2 * b + 1 : 2 * b + 2, :] = place[:, 128:]
        seen = seen + count[:, 255:256]

    slot_row = lax.broadcasted_iota(jnp.int32, (HALF, 128), 0).astype(F32)

    def fill_slots(t, carry):
        columns = pl.ds(pl.multiple_of(t * 128, 128), 128)
        here = z_pos[pl.ds(t, 1), :] == slot_row
        for target, first, second in ((slot_a, 0, 2), (slot_b, 4, 6)):
            for piece in range(2):
                for rows_at, which in ((0, first), (HALF, second)):
                    value = z_val[which + piece, pl.ds(t, 1), :]
                    target[piece, rows_at : rows_at + HALF, columns] = jnp.where(
                        here, value, 0.0
                    ).astype(BF16)
        return carry

    lax.fori_loop(0, TILES, fill_slots, 0, unroll=2)
    for i, source in enumerate((slot_a, slot_b)):
        total = jnp.zeros((DEV, 128), F32)
        for piece in range(2):
            total = total + lax.dot_general(
                chosen[...], source[piece], (((1,), (1,)), ((), ())), preferred_element_type=F32
            )
        out_slots[i] = total

    def add_pressure(k, heavy):
        at = pl.multiple_of(k * 8, 8)
        temp, salt = st[pl.ds(at, 8), :], st[pl.ds(128 + at, 8), :]
        heavy = heavy + jnp.where(k < level, 0.8 * salt - 0.2 * temp, 0.0)
        pres[pl.ds(at, 8), :] = 0.1 * heavy
        return heavy

    lax.fori_loop(0, NZ, add_pressure, jnp.zeros((8, 128), F32), unroll=4)
    level_f = level.astype(F32)
    is_top = oy == N_OY - 1
    backward = 127 - lane
    for i in range(10):
        source, base = (st, 64 * i) if i < 8 else (pres, 64 * (i - 8))
        part = pl.ds(8 * i, 8)
        south_out[part, :] = source[pl.ds(base, 8, stride=8), :]
        top = source[pl.ds(base + 7, 8, stride=8), :]
        mirrored = jnp.take_along_axis(top, backward, axis=1)
        if 4 <= i < 8:
            mirrored = -mirrored
        north_out[part, :] = jnp.where(is_top, mirrored, top)
    top = jnp.broadcast_to(level_f[7:8, :], (8, 128))
    mirrored = jnp.take_along_axis(top, backward, axis=1)
    north_out[80:88, :] = jnp.where(is_top, mirrored, top)
    south_out[80:88, :] = jnp.broadcast_to(level_f[0:1, :], (8, 128))

    def pack_columns(k, packed):
        west, east = packed
        at = pl.multiple_of(k * 8, 8)
        for f in range(5):
            source, base = (st, 128 * f) if f < 4 else (pres, 0)
            plane = source[pl.ds(base + at, 8), :]
            place = 16 * f + k
            west = jnp.where(lane == place, pltpu.roll(plane, place, 1), west)
            east = jnp.where(lane == place, pltpu.roll(plane, place + 1, 1), east)
        return west, east

    none = jnp.zeros((8, 128), F32)
    west, east = lax.fori_loop(0, NZ, pack_columns, (none, none), unroll=2)
    west_out[...] = jnp.where(lane == 80, pltpu.roll(level_f, 80, 1), west)
    east_out[...] = jnp.where(lane == 80, pltpu.roll(level_f, 81, 1), east)

    pl.semaphore_wait(barrier, DEV - 1)
    for mask in PARTNERS:
        partner = me ^ mask
        pltpu.make_async_remote_copy(
            out_slots.at[:, pl.ds(partner, 1)], in_slots.at[:, pl.ds(me, 1)],
            out_sem.at[0], in_sem.at[0], device_id=partner, device_id_type=LOGICAL,
        ).start()
    own_slots = pltpu.make_async_copy(
        out_slots.at[:, pl.ds(me, 1)], in_slots.at[:, pl.ds(me, 1)], local_sem.at[0]
    )
    own_slots.start()

    def halo(source, target, out_at, in_at, device):
        return pltpu.make_async_remote_copy(
            source, target, halo_out_sem.at[out_at], halo_in_sem.at[in_at],
            device_id=device, device_id_type=LOGICAL,
        )

    to_west = halo(west_out, side_in.at[0], 2, 2, lax.rem(ox + n_ox - 1, n_ox) * N_OY + oy)
    to_east = halo(east_out, side_in.at[1], 3, 3, lax.rem(ox + 1, n_ox) * N_OY + oy)
    above = jnp.where(is_top, me ^ (DEV - N_OY), me + 1)
    lands = jnp.where(is_top, 0, 1)
    to_north = halo(north_out, halo_in.at[lands], 0, lands, above)
    to_south = halo(south_out, halo_in.at[0], 1, 0, me - 1)
    to_west.start()
    to_east.start()
    to_north.start()

    @pl.when(oy > 0)
    def _():
        to_south.start()

    def everything(buffers, which):
        source, target = buffers
        if which == 0:
            source, target = source.at[:, pl.ds(0, DEV - 1)], target.at[:, pl.ds(0, DEV - 1)]
        else:
            source, target = source.at[pl.ds(0, DEV - 1)], target.at[pl.ds(0, DEV - 1)]
        return pltpu.make_async_remote_copy(
            source, target, out_sem.at[which], in_sem.at[which],
            device_id=me ^ 1, device_id_type=LOGICAL,
        )

    slots_moved = everything((out_slots, in_slots), 0)
    slots_moved.wait_recv()
    own_slots.wait()

    for i in range(8):
        a, b = pl.ds(8 * i, 8), pl.ds(HALF + 8 * i, 8)
        for plane, first, second in ((0, 0, 2), (1, 4, None)):
            one, two = in_slots[plane, a, :], in_slots[plane, b, :]
            head = jnp.where(low_half, one, pltpu.roll(two, HALF, 1))
            tail = jnp.where(low_half, pltpu.roll(one, HALF, 1), two)
            rows[first, a, :], rows[first + 1, a, :] = split(head)
            if second is not None:
                rows[second, a, :], rows[second + 1, a, :] = split(tail)
            else:
                rows[6, a, :] = tail
    column_row = lax.broadcasted_iota(jnp.int32, (128, 128), 0)

    def mark_cells(r, carry):
        columns = pl.ds(pl.multiple_of(r * 128, 128), 128)
        place = rows[6, pl.ds(r, 1), :].astype(jnp.int32)
        right[:, columns] = jnp.where((place & 127) == column_row, 1.0, 0.0).astype(BF16)
        mine = (place >> 7) == (sub & 3)
        stack = []
        for value in range(3):
            high, low = rows[2 * value, pl.ds(r, 1), :], rows[2 * value + 1, pl.ds(r, 1), :]
            stack.append(jnp.where(mine, jnp.where(sub < 4, high, low), 0.0))
        stack.append(none)
        left[:, columns] = jnp.concatenate(stack, axis=0).astype(BF16)
        return carry

    lax.fori_loop(0, HALF, mark_cells, 0, unroll=4)
    sums = lax.dot_general(
        left[...], right[...], (((1,), (1,)), ((), ())), preferred_element_type=F32
    )
    total_t, total_s, total_w = (
        part + pltpu.roll(part, 4, 0) for part in (sums[0:8], sums[8:16], sums[16:24])
    )
    divisor = jnp.maximum(total_w, 1.0)
    heat_flux = atm[1] * (atm[0] - total_t / divisor)
    fresh_flux = atm[2] * (total_s / divisor)
    for i in range(TILES):
        part = pl.ds(8 * i, 8)
        plane = in_slots[1, part, :]
        place = jnp.where(low_half, pltpu.roll(plane, HALF, 1), plane).astype(jnp.int32)
        column, chunk = place & 127, place >> 7
        picked = none
        for h in range(4):
            heat = jnp.take_along_axis(
                jnp.broadcast_to(heat_flux[h : h + 1, :], (8, 128)), column, axis=1
            )
            fresh = jnp.take_along_axis(
                jnp.broadcast_to(fresh_flux[h : h + 1, :], (8, 128)), column, axis=1
            )
            picked = jnp.where(chunk == h, jnp.where(low_half, heat, fresh), picked)
        out_flux[part, :] = picked

    for mask in PARTNERS:
        partner = me ^ mask
        pltpu.make_async_remote_copy(
            out_flux.at[pl.ds(partner, 1)], in_flux.at[pl.ds(me, 1)],
            out_sem.at[1], in_sem.at[1], device_id=partner, device_id_type=LOGICAL,
        ).start()
    own_flux = pltpu.make_async_copy(
        out_flux.at[pl.ds(me, 1)], in_flux.at[pl.ds(me, 1)], local_sem.at[1]
    )
    own_flux.start()

    halo(west_out, side_in.at[0], 2, 2, me).wait_recv()
    halo(east_out, side_in.at[1], 3, 3, me).wait_recv()
    halo(north_out, halo_in.at[0], 0, 0, me).wait_recv()

    @pl.when(oy > 0)
    def _():
        halo(north_out, halo_in.at[1], 0, 1, me).wait_recv()

    @pl.when(oy == 0)
    def _():
        halo_in[1] = jnp.zeros((PLANES, 128), F32)

    from_east, from_west = side_in[0], side_in[1]

    def around(plane, place):
        return (
            jnp.where(lane == 127, pltpu.roll(from_east, 127 - place, 1), pltpu.roll(plane, 127, 1)),
            jnp.where(lane == 0, pltpu.roll(from_west, 128 - place, 1), pltpu.roll(plane, 1, 1)),
            jnp.where(sub == 7, halo_in[0, pl.ds(place, 1), :], pltpu.roll(plane, 7, 0)),
            jnp.where(sub == 0, halo_in[1, pl.ds(place, 1), :], pltpu.roll(plane, 1, 0)),
        )

    levels_near = around(level_f, 80)
    row_at = (oy * CY + sub).astype(F32)
    coriolis = 0.2 + 0.8 * row_at / (CY * N_OY)

    def step(k, carry):
        depth = k.astype(F32)
        at = pl.multiple_of(k * 8, 8)
        up = pl.multiple_of(jnp.maximum(k - 1, 0) * 8, 8)
        down = pl.multiple_of(jnp.minimum(k + 1, NZ - 1) * 8, 8)
        wet = (depth < level_f).astype(F32)
        wet_near = [(depth < near).astype(F32) for near in levels_near]
        wet_down = jnp.where(k < NZ - 1, (depth + 1.0 < level_f).astype(F32), 0.0)
        wet_up = jnp.where(k > 0, (depth - 1.0 < level_f).astype(F32), 0.0)

        def spread(plane, place):
            total = none
            for near, mask in zip(around(plane, place), wet_near):
                total = total + mask * (near - plane)
            return wet * total

        for f in range(2):
            base = 128 * f
            plane = st[pl.ds(base + at, 8), :]
            over, under = st[pl.ds(base + up, 8), :], st[pl.ds(base + down, 8), :]
            vertical = wet * (wet_down * (under - plane) + wet_up * (over - plane))
            out[pl.ds(base + at, 8), :] = wet * (
                plane + EDDY_KAPPA * (spread(plane, 16 * f + k) + vertical)
            )
        p = pres[pl.ds(at, 8), :]
        p_e, p_w, p_n, p_s = around(p, 64 + k)
        grad_x = 0.5 * (wet_near[0] * (p_e - p) + wet_near[1] * (p - p_w))
        grad_y = 0.5 * (wet_near[2] * (p_n - p) + wet_near[3] * (p - p_s))
        u, v = st[pl.ds(256 + at, 8), :], st[pl.ds(384 + at, 8), :]
        out[pl.ds(256 + at, 8), :] = wet * (
            u + STEP * (coriolis * v - grad_x) + VISC * spread(u, 32 + k)
        )
        out[pl.ds(384 + at, 8), :] = wet * (
            v + STEP * (-coriolis * u - grad_y) + VISC * spread(v, 48 + k)
        )
        return carry

    lax.fori_loop(0, NZ, step, 0, unroll=2)

    flux_moved = everything((out_flux, in_flux), 1)
    flux_moved.wait_recv()
    own_flux.wait()

    flipped[...] = in_flux[...].T
    owners = [z_own[8 * c : 8 * c + 8, :] for c in range(2)]
    places = [z_pos[8 * c : 8 * c + 8, :] for c in range(2)]
    found = [[none, none], [none, none]]
    for s in range(SLOTS):
        for c in range(2):
            here = places[c] == float(s)
            for v in range(2):
                table = jnp.broadcast_to(flipped[HALF * v + s : HALF * v + s + 1, :], (8, 128))
                found[v][c] = jnp.where(
                    here, jnp.take_along_axis(table, owners[c], axis=1), found[v][c]
                )
    area_0, area_1 = z_area[0:8, :], z_area[8:16, :]
    share = SEA_TOP * wet_top / (area_0 + area_1)
    for v in range(2):
        surface = (area_0 * found[v][0] + area_1 * found[v][1]) * share
        out[128 * v : 128 * v + 8, :] = out[128 * v : 128 * v + 8, :] + surface

    slots_moved.wait_send()
    flux_moved.wait_send()
    to_west.wait_send()
    to_east.wait_send()
    to_north.wait_send()

    @pl.when(oy > 0)
    def _():
        to_south.wait_send()


def per_device(state, levels, owner, atm_cell, area, air_temp, exchange_rate, rainfall):
    any_space = pl.BlockSpec(memory_space=pl.ANY)
    result = pl.pallas_call(
        kernel,
        out_shape=jax.ShapeDtypeStruct((4 * NZ * CY, CX), F32),
        in_specs=[any_space] * 8,
        out_specs=pl.BlockSpec(memory_space=pltpu.VMEM),
        scratch_shapes=[
            pltpu.VMEM((512, 128), F32),
            pltpu.VMEM((8, 128), jnp.int32),
            pltpu.VMEM((TILES, 128), jnp.int32),
            pltpu.VMEM((TILES, 128), jnp.int32),
            pltpu.VMEM((TILES, 128), F32),
            pltpu.VMEM((3, 8, 128), F32),
            pltpu.VMEM((TILES, 128), jnp.int32),
            pltpu.VMEM((TILES, 128), jnp.int32),
            pltpu.VMEM((TILES, 128), F32),
            pltpu.VMEM((TILES, 128), F32),
            pltpu.VMEM((8, TILES, 128), F32),
            pltpu.VMEM((DEV, TILES * 128), BF16),
            pltpu.VMEM((2, 128, TILES * 128), BF16),
            pltpu.VMEM((2, 128, TILES * 128), BF16),
            pltpu.VMEM((2, DEV, 128), F32),
            pltpu.VMEM((2, DEV, 128), F32),
            pltpu.VMEM((DEV, 128), F32),
            pltpu.VMEM((DEV, 128), F32),
            pltpu.VMEM((128, 128), F32),
            pltpu.VMEM((7, HALF, 128), F32),
            pltpu.VMEM((32, HALF * 128), BF16),
            pltpu.VMEM((128, HALF * 128), BF16),
            pltpu.VMEM((128, 128), F32),
            pltpu.VMEM((PLANES, 128), F32),
            pltpu.VMEM((PLANES, 128), F32),
            pltpu.VMEM((2, PLANES, 128), F32),
            pltpu.VMEM((8, 128), F32),
            pltpu.VMEM((8, 128), F32),
            pltpu.VMEM((2, 8, 128), F32),
            pltpu.SemaphoreType.DMA((11,)),
            pltpu.SemaphoreType.DMA((2,)),
            pltpu.SemaphoreType.DMA((2,)),
            pltpu.SemaphoreType.DMA((4,)),
            pltpu.SemaphoreType.DMA((4,)),
        ],
        compiler_params=pltpu.CompilerParams(
            collective_id=0, has_side_effects=True, vmem_limit_bytes=60 * 1024 * 1024
        ),
    )(
        state.reshape(4 * NZ * CY, CX),
        levels,
        owner.reshape(TILES, 128),
        atm_cell.reshape(TILES, 128),
        area.reshape(TILES, 128),
        air_temp.reshape(4, 128),
        exchange_rate.reshape(4, 128),
        rainfall.reshape(4, 128),
    )
    return result.reshape(4, NZ, CY, CX)


def solution(mesh):
    entries = P(("ox", "oy"))
    in_specs = (
        P(None, None, "oy", "ox"),
        P("oy", "ox"),
        P(("ox", "oy"), None),
        entries,
        entries,
        entries,
        entries,
        entries,
    )
    return jax.shard_map(
        per_device,
        mesh=mesh,
        in_specs=in_specs,
        out_specs=P(None, None, "oy", "ox"),
        check_vma=False,
    )
```

time: 147 us -> 27.7 us (0.19)
  matrix products: 53.9 us -> 0 us
  starting transfers between devices: 40 us -> 0 us
  local copies, waits for them, and re-layouts: 27.9 us -> 1.67 us
  Pallas kernels: 0 us -> 25.9 us
  waiting for transfers between devices: 16.4 us -> 0 us
  other arithmetic: 6.62 us -> 0 us
    dot_general x36 -> x0, matrix products: 53.9 us -> none  [the longest x16 30.4 us: pick_block(): jnp.dot(onehot, table, precision=lax.Precision.HIGHEST, preferred_element...]
    all_to_all x4 -> x0, starting transfers between devices: 33.5 us -> none  [the longest x1 9.76 us: per_device(): lax.all_to_all(returning, ('ox', 'oy'), split_axis=0, concat_axis=0, tile...]
    pallas_call x0 -> x1, Pallas kernels: none -> 25.9 us  [per_device(): pl.pallas_call(kernel, out_shape=jax.ShapeDtypeStruct((4 * NZ * CY, CX),...]
    all_to_all x4 -> x0, waiting for transfers between devices: 16.4 us -> none  [the longest x1 9.7 us: per_device(): lax.all_to_all(returning, ('ox', 'oy'), split_axis=0, concat_axis=0, tile...]
    scatter x1 -> x0, local copies, waits for them, and re-layouts: 14.4 us -> none  [per_device(): haloed_grid_array.at[:, row_count + 1, 1:col_count + 1]]
    ppermute x4 -> x0, starting transfers between devices: 6.54 us -> none  [the longest x2 5.25 us: extended(): lax.ppermute(lax.slice_in_dim(block, block.shape[dim] - width, None, axis...]
    another operation x8 -> x0, local copies, waits for them, and re-layouts: 2.06 us -> none  [the longest x1 0.71 us: per_device(): sea_salt = jnp.repeat(state[1, 0].reshape(-1), 2)]
    reshape x7 -> x0, local copies, waits for them, and re-layouts: 1.64 us -> none  [the longest x1 0.46 us: per_device(): pair_area = area.reshape(row_count, col_count, 2)]
  transfers between devices with their start and end apart: 8 -> 0, of which waited for: 2 -> 0; matrix products, arithmetic and copies ran while one was open for 28% -> 0% of each run, Pallas kernels for 0% -> 0%
where the time goes in v1:
time: 27.7 us; the launch traced here: 27.6 us
  Pallas kernels  25.9 us (94%)
  local copies, waits for them, and re-layouts  1.67 us (6%)
    pallas_call x1, Pallas kernels, per_device(): pl.pallas_call(kernel, out_shape=jax.ShapeDtypeStruct((4 * NZ * CY, CX),...  25.9 us
    unnamed x1, local copies, waits for them, and re-layouts  1.67 us

profile of v1, /device:TPU:1, one launch (start us, length us, event | category | flops | bytes accessed | tf_op | source)
XLA Modules:
  0.0 27.6 jit_solution(6834573650530677081)
XLA Ops:
  0.0 25.9 %shard_map.82 = f32[512,128]{1,0:T(8,128)} custom-call(f32[512,128]{1,0:T(8,128)} %bitcast.9, s32[8,128]{1,0:T(8,128)} %levels.1, s32[16,128]{1,0:T(8,128)} %bitcast.10, s32[16,128]{1,0:T(8,128)} %bitcast.11, f32[16,128]{1,0:T(8,128)} %bitcast.12, f32[4,128]{1,0:T(4,128)} %bitcast.13, f32[4,128]{1,0:T(4,128)} %bitcast.14, f32[4,128]{1,0:T(4,128)} %bitcast.15), custom_call_target="tpu_custom_call" | custom-call | tf_op jit(solution)/shard_map/pallas_call | solution.py:396
  25.9 1.7 %copy.10 = f32[4,16,8,128]{3,2,1,0:T(8,128)} copy(f32[4,16,8,128]{3,2,1,0:T(8,128)} %bitcast.8) | data formatting | bytes 524288

commit v2 on v1

--- a/solution.py
+++ b/solution.py
@@ -13,6 +13,7 @@
 TILES = 16
 HALF = 64
 SLOTS = 48
+GROUP = 8
 PLANES = 88
 EDDY_KAPPA = 0.1
 VISC = 0.1
@@ -43,7 +44,7 @@
     z_own, z_cell, z_pos, z_area, z_val,
     chosen, slot_a, slot_b,
     out_slots, in_slots, out_flux, in_flux, flipped,
-    rows, left, right,
+    rows,
     pres, north_out, south_out, halo_in, west_out, east_out, side_in,
     local_sem, out_sem, in_sem, halo_out_sem, halo_in_sem,
 ):
@@ -62,11 +63,11 @@
             )
         )
     ]
-    for copy in loads:
-        copy.start()
     barrier = pltpu.get_barrier_semaphore()
     for mask in PARTNERS:
         pl.semaphore_signal(barrier, inc=1, device_id=me ^ mask, device_id_type=LOGICAL)
+    for copy in loads:
+        copy.start()
     for copy in loads:
         copy.wait()
 
@@ -141,6 +142,18 @@
                 chosen[...], source[piece], (((1,), (1,)), ((), ())), preferred_element_type=F32
             )
         out_slots[i] = total
+
+    pl.semaphore_wait(barrier, DEV - 1)
+    for mask in PARTNERS:
+        partner = me ^ mask
+        pltpu.make_async_remote_copy(
+            out_slots.at[:, pl.ds(partner, 1)], in_slots.at[:, pl.ds(me, 1)],
+            out_sem.at[0], in_sem.at[0], device_id=partner, device_id_type=LOGICAL,
+        ).start()
+    own_slots = pltpu.make_async_copy(
+        out_slots.at[:, pl.ds(me, 1)], in_slots.at[:, pl.ds(me, 1)], local_sem.at[0]
+    )
+    own_slots.start()
 
     def add_pressure(k, heavy):
         at = pl.multiple_of(k * 8, 8)
@@ -183,18 +196,6 @@
     west_out[...] = jnp.where(lane == 80, pltpu.roll(level_f, 80, 1), west)
     east_out[...] = jnp.where(lane == 80, pltpu.roll(level_f, 81, 1), east)
 
-    pl.semaphore_wait(barrier, DEV - 1)
-    for mask in PARTNERS:
-        partner = me ^ mask
-        pltpu.make_async_remote_copy(
-            out_slots.at[:, pl.ds(partner, 1)], in_slots.at[:, pl.ds(me, 1)],
-            out_sem.at[0], in_sem.at[0], device_id=partner, device_id_type=LOGICAL,
-        ).start()
-    own_slots = pltpu.make_async_copy(
-        out_slots.at[:, pl.ds(me, 1)], in_slots.at[:, pl.ds(me, 1)], local_sem.at[0]
-    )
-    own_slots.start()
-
     def halo(source, target, out_at, in_at, device):
         return pltpu.make_async_remote_copy(
             source, target, halo_out_sem.at[out_at], halo_in_sem.at[in_at],
@@ -241,27 +242,28 @@
                 rows[second, a, :], rows[second + 1, a, :] = split(tail)
             else:
                 rows[6, a, :] = tail
-    column_row = lax.broadcasted_iota(jnp.int32, (128, 128), 0)
-
-    def mark_cells(r, carry):
-        columns = pl.ds(pl.multiple_of(r * 128, 128), 128)
-        place = rows[6, pl.ds(r, 1), :].astype(jnp.int32)
-        right[:, columns] = jnp.where((place & 127) == column_row, 1.0, 0.0).astype(BF16)
-        mine = (place >> 7) == (sub & 3)
-        stack = []
-        for value in range(3):
-            high, low = rows[2 * value, pl.ds(r, 1), :], rows[2 * value + 1, pl.ds(r, 1), :]
-            stack.append(jnp.where(mine, jnp.where(sub < 4, high, low), 0.0))
-        stack.append(none)
-        left[:, columns] = jnp.concatenate(stack, axis=0).astype(BF16)
-        return carry
-
-    lax.fori_loop(0, HALF, mark_cells, 0, unroll=4)
-    sums = lax.dot_general(
-        left[...], right[...], (((1,), (1,)), ((), ())), preferred_element_type=F32
-    )
+    column_row = lax.broadcasted_iota(jnp.int32, (HALF, 128), 0)
+    sums = jnp.zeros((48, HALF), F32)
+    for start in range(0, HALF, GROUP):
+        lefts, rights = [], []
+        for r in range(start, start + GROUP):
+            place = rows[6, r : r + 1, :].astype(jnp.int32)
+            rights.append(jnp.where((place & 63) == column_row, 1.0, 0.0).astype(BF16))
+            mine = (((place >> 7) & 3) + ((place >> 4) & 4)) == sub
+            lefts.append(
+                jnp.concatenate(
+                    [jnp.where(mine, rows[i, r : r + 1, :], 0.0) for i in range(6)], axis=0
+                ).astype(BF16)
+            )
+        sums = sums + lax.dot_general(
+            jnp.concatenate(lefts, axis=1),
+            jnp.concatenate(rights, axis=1),
+            (((1,), (1,)), ((), ())),
+            preferred_element_type=F32,
+        )
     total_t, total_s, total_w = (
-        part + pltpu.roll(part, 4, 0) for part in (sums[0:8], sums[8:16], sums[16:24])
+        jnp.concatenate([part, pltpu.roll(part, 4, 0)], axis=1)
+        for part in (sums[16 * i : 16 * i + 8] + sums[16 * i + 8 : 16 * i + 16] for i in range(3))
     )
     divisor = jnp.maximum(total_w, 1.0)
     heat_flux = atm[1] * (atm[0] - total_t / divisor)
@@ -395,7 +397,7 @@
     any_space = pl.BlockSpec(memory_space=pl.ANY)
     result = pl.pallas_call(
         kernel,
-        out_shape=jax.ShapeDtypeStruct((4 * NZ * CY, CX), F32),
+        out_shape=pltpu.VMEM((4 * NZ * CY, CX), F32),
         in_specs=[any_space] * 8,
         out_specs=pl.BlockSpec(memory_space=pltpu.VMEM),
         scratch_shapes=[
@@ -419,8 +421,6 @@
             pltpu.VMEM((DEV, 128), F32),
             pltpu.VMEM((128, 128), F32),
             pltpu.VMEM((7, HALF, 128), F32),
-            pltpu.VMEM((32, HALF * 128), BF16),
-            pltpu.VMEM((128, HALF * 128), BF16),
             pltpu.VMEM((128, 128), F32),
             pltpu.VMEM((PLANES, 128), F32),
             pltpu.VMEM((PLANES, 128), F32),
@@ -435,7 +435,7 @@
             pltpu.SemaphoreType.DMA((4,)),
         ],
         compiler_params=pltpu.CompilerParams(
-            collective_id=0, has_side_effects=True, vmem_limit_bytes=60 * 1024 * 1024
+            collective_id=0, has_side_effects=True, vmem_limit_bytes=56 * 1024 * 1024
         ),
     )(
         state.reshape(4 * NZ * CY, CX),

time: 27.7 us -> 24.6 us (0.89)
  Pallas kernels: 25.9 us -> 23.7 us
  local copies, waits for them, and re-layouts: 1.67 us -> 0.71 us
    pallas_call x1, Pallas kernels: 25.9 us -> 23.7 us  [per_device(): pl.pallas_call(kernel, out_shape=pltpu.VMEM((4 * NZ * CY, CX), F32), in_s...]
    unnamed x1, local copies, waits for them, and re-layouts: 1.67 us -> 0.71 us
where the time goes in v2:
time: 24.6 us; the launch traced here: 24.5 us
  Pallas kernels  23.7 us (96%)
  local copies, waits for them, and re-layouts  0.71 us (3%)
    pallas_call x1, Pallas kernels, per_device(): pl.pallas_call(kernel, out_shape=pltpu.VMEM((4 * NZ * CY, CX), F32), in_s...  23.7 us
    unnamed x1, local copies, waits for them, and re-layouts  0.71 us

profile of v2, /device:TPU:1, one launch (start us, length us, event | category | flops | bytes accessed | tf_op | source)
XLA Modules:
  0.0 24.5 jit_solution(5962979955896392916)
XLA Ops:
  0.0 23.7 %shard_map.82 = f32[512,128]{1,0:T(8,128)S(1)} custom-call(f32[512,128]{1,0:T(8,128)} %bitcast.9, s32[8,128]{1,0:T(8,128)} %levels.1, s32[16,128]{1,0:T(8,128)} %bitcast.10, s32[16,128]{1,0:T(8,128)} %bitcast.11, f32[16,128]{1,0:T(8,128)} %bitcast.12, f32[4,128]{1,0:T(4,128)} %bitcast.13, f32[4,128]{1,0:T(4,128)} %bitcast.14, f32[4,128]{1,0:T(4,128)} %bitcast.15), custom_call_target="tpu_custom_call" | custom-call | tf_op jit(solution)/shard_map/pallas_call | solution.py:398
  23.8 0.7 %copy.10 = f32[4,16,8,128]{3,2,1,0:T(8,128)} copy(f32[4,16,8,128]{3,2,1,0:T(8,128)S(1)} %bitcast.8) | data formatting | bytes 524288

commit v3 on v2

--- a/solution.py
+++ b/solution.py
@@ -29,7 +29,9 @@
     return 4 * (ring[mask & 3] + ring[(mask >> 3) & 3] + ring[(mask >> 5) & 3]) + ((mask >> 2) & 1)
 
 
-PARTNERS = sorted(range(1, DEV), key=lambda mask: -hops(mask))
+PARTNERS = sorted(range(1, DEV), key=lambda mask: -(hops(mask) // 4))
+SENDS = sorted(range(DEV - 1, 0, -1), key=lambda mask: -(hops(mask) // 4))
+RETURNS = sorted(range(DEV - 1, 0, -1), key=lambda mask: -(hops(mask) // 4))
 
 
 def split(value):
@@ -144,7 +146,7 @@
         out_slots[i] = total
 
     pl.semaphore_wait(barrier, DEV - 1)
-    for mask in PARTNERS:
+    for mask in SENDS:
         partner = me ^ mask
         pltpu.make_async_remote_copy(
             out_slots.at[:, pl.ds(partner, 1)], in_slots.at[:, pl.ds(me, 1)],
@@ -284,7 +286,7 @@
             picked = jnp.where(chunk == h, jnp.where(low_half, heat, fresh), picked)
         out_flux[part, :] = picked
 
-    for mask in PARTNERS:
+    for mask in RETURNS:
         partner = me ^ mask
         pltpu.make_async_remote_copy(
             out_flux.at[pl.ds(partner, 1)], in_flux.at[pl.ds(me, 1)],
@@ -368,14 +370,34 @@
     owners = [z_own[8 * c : 8 * c + 8, :] for c in range(2)]
     places = [z_pos[8 * c : 8 * c + 8, :] for c in range(2)]
     found = [[none, none], [none, none]]
+    pieces = []
+    for v in (1,):
+        high, low = split(flipped[HALF * v : HALF * v + SLOTS, :])
+        pieces += [high.astype(BF16), low.astype(BF16)]
+    pieces = jnp.concatenate(pieces, axis=0)
+    slot_at = lax.broadcasted_iota(jnp.int32, (SLOTS, 128), 0).astype(F32)
+    for b in range(TILES // 2):
+        near = jnp.dot(pieces, chosen[:, 256 * b : 256 * (b + 1)], preferred_element_type=F32)
+        for half in range(2):
+            t = 2 * b + half
+            here = z_pos[t : t + 1, :] == slot_at
+            columns = slice(128 * half, 128 * (half + 1))
+            for i, v in enumerate((1,)):
+                at = 2 * SLOTS * i
+                both = near[at : at + SLOTS, columns] + near[at + SLOTS : at + 2 * SLOTS, columns]
+                z_val[v, t : t + 1, :] = jnp.sum(
+                    jnp.where(here, both, 0.0), axis=0, keepdims=True
+                )
     for s in range(SLOTS):
         for c in range(2):
             here = places[c] == float(s)
-            for v in range(2):
+            for v in (0,):
                 table = jnp.broadcast_to(flipped[HALF * v + s : HALF * v + s + 1, :], (8, 128))
                 found[v][c] = jnp.where(
                     here, jnp.take_along_axis(table, owners[c], axis=1), found[v][c]
                 )
+    for v in (1,):
+        found[v] = [z_val[v, 8 * c : 8 * c + 8, :] for c in range(2)]
     area_0, area_1 = z_area[0:8, :], z_area[8:16, :]
     share = SEA_TOP * wet_top / (area_0 + area_1)
     for v in range(2):

time: 24.6 us -> 24.2 us (0.984)
  Pallas kernels: 23.7 us -> 23.3 us
    pallas_call x1, Pallas kernels: 23.7 us -> 23.3 us  [per_device(): pl.pallas_call(kernel, out_shape=pltpu.VMEM((4 * NZ * CY, CX), F32), in_s...]
where the time goes in v3:
time: 24.2 us; the launch traced here: 24 us
  Pallas kernels  23.3 us (96%)
  local copies, waits for them, and re-layouts  0.71 us (3%)
    pallas_call x1, Pallas kernels, per_device(): pl.pallas_call(kernel, out_shape=pltpu.VMEM((4 * NZ * CY, CX), F32), in_s...  23.3 us
    unnamed x1, local copies, waits for them, and re-layouts  0.71 us

profile of v3, /device:TPU:1, one launch (start us, length us, event | category | flops | bytes accessed | tf_op | source)
XLA Modules:
  0.0 24.0 jit_solution(16385113808073261461)
XLA Ops:
  0.0 23.3 %shard_map.82 = f32[512,128]{1,0:T(8,128)S(1)} custom-call(f32[512,128]{1,0:T(8,128)} %bitcast.9, s32[8,128]{1,0:T(8,128)} %levels.1, s32[16,128]{1,0:T(8,128)} %bitcast.10, s32[16,128]{1,0:T(8,128)} %bitcast.11, f32[16,128]{1,0:T(8,128)} %bitcast.12, f32[4,128]{1,0:T(4,128)} %bitcast.13, f32[4,128]{1,0:T(4,128)} %bitcast.14, f32[4,128]{1,0:T(4,128)} %bitcast.15), custom_call_target="tpu_custom_call" | custom-call | tf_op jit(solution)/shard_map/pallas_call | solution.py:420
  23.3 0.7 %copy.10 = f32[4,16,8,128]{3,2,1,0:T(8,128)} copy(f32[4,16,8,128]{3,2,1,0:T(8,128)S(1)} %bitcast.8) | data formatting | bytes 524288

commit v4 on v3

--- a/solution.py
+++ b/solution.py
@@ -66,10 +66,12 @@
         )
     ]
     barrier = pltpu.get_barrier_semaphore()
-    for mask in PARTNERS:
+    for mask in PARTNERS[:44]:
         pl.semaphore_signal(barrier, inc=1, device_id=me ^ mask, device_id_type=LOGICAL)
     for copy in loads:
         copy.start()
+    for mask in PARTNERS[44:]:
+        pl.semaphore_signal(barrier, inc=1, device_id=me ^ mask, device_id_type=LOGICAL)
     for copy in loads:
         copy.wait()
 
@@ -270,21 +272,19 @@
     divisor = jnp.maximum(total_w, 1.0)
     heat_flux = atm[1] * (atm[0] - total_t / divisor)
     fresh_flux = atm[2] * (total_s / divisor)
-    for i in range(TILES):
-        part = pl.ds(8 * i, 8)
-        plane = in_slots[1, part, :]
-        place = jnp.where(low_half, pltpu.roll(plane, HALF, 1), plane).astype(jnp.int32)
+    for i in range(TILES // 2):
+        a, b = pl.ds(8 * i, 8), pl.ds(HALF + 8 * i, 8)
+        place = rows[6, a, :].astype(jnp.int32)
         column, chunk = place & 127, place >> 7
-        picked = none
+        heat, fresh = none, none
         for h in range(4):
-            heat = jnp.take_along_axis(
-                jnp.broadcast_to(heat_flux[h : h + 1, :], (8, 128)), column, axis=1
-            )
-            fresh = jnp.take_along_axis(
-                jnp.broadcast_to(fresh_flux[h : h + 1, :], (8, 128)), column, axis=1
-            )
-            picked = jnp.where(chunk == h, jnp.where(low_half, heat, fresh), picked)
-        out_flux[part, :] = picked
+            here = chunk == h
+            table = jnp.broadcast_to(heat_flux[h : h + 1, :], (8, 128))
+            heat = jnp.where(here, jnp.take_along_axis(table, column, axis=1), heat)
+            table = jnp.broadcast_to(fresh_flux[h : h + 1, :], (8, 128))
+            fresh = jnp.where(here, jnp.take_along_axis(table, column, axis=1), fresh)
+        out_flux[a, :] = jnp.where(low_half, heat, pltpu.roll(fresh, HALF, 1))
+        out_flux[b, :] = jnp.where(low_half, pltpu.roll(heat, HALF, 1), fresh)
 
     for mask in RETURNS:
         partner = me ^ mask
@@ -314,7 +314,7 @@
     def around(plane, place):
         return (
             jnp.where(lane == 127, pltpu.roll(from_east, 127 - place, 1), pltpu.roll(plane, 127, 1)),
-            jnp.where(lane == 0, pltpu.roll(from_west, 128 - place, 1), pltpu.roll(plane, 1, 1)),
+            jnp.where(lane == 0, pltpu.roll(from_west, (128 - place) & 127, 1), pltpu.roll(plane, 1, 1)),
             jnp.where(sub == 7, halo_in[0, pl.ds(place, 1), :], pltpu.roll(plane, 7, 0)),
             jnp.where(sub == 0, halo_in[1, pl.ds(place, 1), :], pltpu.roll(plane, 1, 0)),
         )

time: 24.2 us -> 24.1 us (level)
  no operation moved by 1% of the time
where the time goes in v4:
time: 24.1 us; the launch traced here: 23.9 us
  Pallas kernels  23.2 us (96%)
  local copies, waits for them, and re-layouts  0.71 us (3%)
    pallas_call x1, Pallas kernels, per_device(): pl.pallas_call(kernel, out_shape=pltpu.VMEM((4 * NZ * CY, CX), F32), in_s...  23.2 us
    unnamed x1, local copies, waits for them, and re-layouts  0.71 us

profile of v4, /device:TPU:1, one launch (start us, length us, event | category | flops | bytes accessed | tf_op | source)
XLA Modules:
  0.0 23.9 jit_solution(12914240176497147409)
XLA Ops:
  0.0 23.2 %shard_map.82 = f32[512,128]{1,0:T(8,128)S(1)} custom-call(f32[512,128]{1,0:T(8,128)} %bitcast.9, s32[8,128]{1,0:T(8,128)} %levels.1, s32[16,128]{1,0:T(8,128)} %bitcast.10, s32[16,128]{1,0:T(8,128)} %bitcast.11, f32[16,128]{1,0:T(8,128)} %bitcast.12, f32[4,128]{1,0:T(4,128)} %bitcast.13, f32[4,128]{1,0:T(4,128)} %bitcast.14, f32[4,128]{1,0:T(4,128)} %bitcast.15), custom_call_target="tpu_custom_call" | custom-call | tf_op jit(solution)/shard_map/pallas_call | solution.py:420
  23.2 0.7 %copy.10 = f32[4,16,8,128]{3,2,1,0:T(8,128)} copy(f32[4,16,8,128]{3,2,1,0:T(8,128)S(1)} %bitcast.8) | data formatting | bytes 524288

commit v5 on v4

--- a/solution.py
+++ b/solution.py
@@ -147,18 +147,6 @@
             )
         out_slots[i] = total
 
-    pl.semaphore_wait(barrier, DEV - 1)
-    for mask in SENDS:
-        partner = me ^ mask
-        pltpu.make_async_remote_copy(
-            out_slots.at[:, pl.ds(partner, 1)], in_slots.at[:, pl.ds(me, 1)],
-            out_sem.at[0], in_sem.at[0], device_id=partner, device_id_type=LOGICAL,
-        ).start()
-    own_slots = pltpu.make_async_copy(
-        out_slots.at[:, pl.ds(me, 1)], in_slots.at[:, pl.ds(me, 1)], local_sem.at[0]
-    )
-    own_slots.start()
-
     def add_pressure(k, heavy):
         at = pl.multiple_of(k * 8, 8)
         temp, salt = st[pl.ds(at, 8), :], st[pl.ds(128 + at, 8), :]
@@ -199,6 +187,18 @@
     west, east = lax.fori_loop(0, NZ, pack_columns, (none, none), unroll=2)
     west_out[...] = jnp.where(lane == 80, pltpu.roll(level_f, 80, 1), west)
     east_out[...] = jnp.where(lane == 80, pltpu.roll(level_f, 81, 1), east)
+
+    pl.semaphore_wait(barrier, DEV - 1)
+    for mask in SENDS:
+        partner = me ^ mask
+        pltpu.make_async_remote_copy(
+            out_slots.at[:, pl.ds(partner, 1)], in_slots.at[:, pl.ds(me, 1)],
+            out_sem.at[0], in_sem.at[0], device_id=partner, device_id_type=LOGICAL,
+        ).start()
+    own_slots = pltpu.make_async_copy(
+        out_slots.at[:, pl.ds(me, 1)], in_slots.at[:, pl.ds(me, 1)], local_sem.at[0]
+    )
+    own_slots.start()
 
     def halo(source, target, out_at, in_at, device):
         return pltpu.make_async_remote_copy(

time: 24.1 us -> 24.1 us (level)
  no operation moved by 1% of the time
where the time goes in v5:
time: 24.1 us; the launch traced here: 23.9 us
  Pallas kernels  23.2 us (96%)
  local copies, waits for them, and re-layouts  0.71 us (3%)
    pallas_call x1, Pallas kernels, per_device(): pl.pallas_call(kernel, out_shape=pltpu.VMEM((4 * NZ * CY, CX), F32), in_s...  23.2 us
    unnamed x1, local copies, waits for them, and re-layouts  0.71 us

profile of v5, /device:TPU:1, one launch (start us, length us, event | category | flops | bytes accessed | tf_op | source)
XLA Modules:
  0.0 23.9 jit_solution(14136526103795272983)
XLA Ops:
  0.0 23.2 %shard_map.82 = f32[512,128]{1,0:T(8,128)S(1)} custom-call(f32[512,128]{1,0:T(8,128)} %bitcast.9, s32[8,128]{1,0:T(8,128)} %levels.1, s32[16,128]{1,0:T(8,128)} %bitcast.10, s32[16,128]{1,0:T(8,128)} %bitcast.11, f32[16,128]{1,0:T(8,128)} %bitcast.12, f32[4,128]{1,0:T(4,128)} %bitcast.13, f32[4,128]{1,0:T(4,128)} %bitcast.14, f32[4,128]{1,0:T(4,128)} %bitcast.15), custom_call_target="tpu_custom_call" | custom-call | tf_op jit(solution)/shard_map/pallas_call | solution.py:420
  23.2 0.7 %copy.10 = f32[4,16,8,128]{3,2,1,0:T(8,128)} copy(f32[4,16,8,128]{3,2,1,0:T(8,128)S(1)} %bitcast.8) | data formatting | bytes 524288

commit v6 on v4

--- a/solution.py
+++ b/solution.py
@@ -246,13 +246,15 @@
                 rows[second, a, :], rows[second + 1, a, :] = split(tail)
             else:
                 rows[6, a, :] = tail
-    column_row = lax.broadcasted_iota(jnp.int32, (HALF, 128), 0)
+    column_row = lax.broadcasted_iota(jnp.int32, (HALF, 128), 0).astype(F32).astype(BF16)
+    one, zero = jnp.ones((HALF, 128), BF16), jnp.zeros((HALF, 128), BF16)
     sums = jnp.zeros((48, HALF), F32)
     for start in range(0, HALF, GROUP):
         lefts, rights = [], []
         for r in range(start, start + GROUP):
             place = rows[6, r : r + 1, :].astype(jnp.int32)
-            rights.append(jnp.where((place & 63) == column_row, 1.0, 0.0).astype(BF16))
+            column = (place & 63).astype(F32).astype(BF16)
+            rights.append(jnp.where(column == column_row, one, zero))
             mine = (((place >> 7) & 3) + ((place >> 4) & 4)) == sub
             lefts.append(
                 jnp.concatenate(

time: 24.1 us -> 24.1 us (level)
  no operation moved by 1% of the time
where the time goes in v6:
time: 24.1 us; the launch traced here: 23.9 us
  Pallas kernels  23.2 us (96%)
  local copies, waits for them, and re-layouts  0.71 us (3%)
    pallas_call x1, Pallas kernels, per_device(): pl.pallas_call(kernel, out_shape=pltpu.VMEM((4 * NZ * CY, CX), F32), in_s...  23.2 us
    unnamed x1, local copies, waits for them, and re-layouts  0.71 us

profile of v6, /device:TPU:1, one launch (start us, length us, event | category | flops | bytes accessed | tf_op | source)
XLA Modules:
  0.0 23.9 jit_solution(16965061183798758769)
XLA Ops:
  0.0 23.2 %shard_map.82 = f32[512,128]{1,0:T(8,128)S(1)} custom-call(f32[512,128]{1,0:T(8,128)} %bitcast.9, s32[8,128]{1,0:T(8,128)} %levels.1, s32[16,128]{1,0:T(8,128)} %bitcast.10, s32[16,128]{1,0:T(8,128)} %bitcast.11, f32[16,128]{1,0:T(8,128)} %bitcast.12, f32[4,128]{1,0:T(4,128)} %bitcast.13, f32[4,128]{1,0:T(4,128)} %bitcast.14, f32[4,128]{1,0:T(4,128)} %bitcast.15), custom_call_target="tpu_custom_call" | custom-call | tf_op jit(solution)/shard_map/pallas_call | solution.py:422
  23.2 0.7 %copy.10 = f32[4,16,8,128]{3,2,1,0:T(8,128)} copy(f32[4,16,8,128]{3,2,1,0:T(8,128)S(1)} %bitcast.8) | data formatting | bytes 524288
